TPU v7x, 32 devices: a whole 2x2x4 slice. The times are simulated.
32 devices in a mesh: gx: 16 (over z, x, core), gy: 2 (over y).
Axes of the slice: x: 2, y: 2, z: 4, core: 2. Of those that a mesh axis runs over, the one named last changes fastest.
Arguments:
- offsets: float32 [3, 16, 16, 512], P(None, 'gx', 'gy'), may hold values from 0 to 1
- masses: float32 [16, 16, 512], P('gx', 'gy'), may hold values from 0.02 to 0.2
- kernel: bfloat16 [36, 2, 36, 16, 1024], P(None, None, None, 'gx', 'gy'), may hold values from -1.2 to 3.2, as said below
Outputs:
- acceleration: float32 [3, 16, 16, 512], P(None, 'gx', 'gy')
Inputs may be any that keep to these rules, and one draw needn't show every extreme that they name: `kernel`: G is Hermitian in the wavevector: the entry at -k (each component modulo the grid) is the complex conjugate of the entry at k; all entries at the zero wavevector are zero.
All inputs are finite; a program needn't handle non-finite values.
Results may differ from a plain program's by a relative error of at most 0.0003.
Values sent between devices are 32-bit elements; how exact they have to be, the bound alone decides.
A program may use at most 128 MiB of HBM per device.

v0:
```python
import math

import jax
import jax.numpy as jnp
from jax import lax
from jax.sharding import PartitionSpec as P

BODIES = 8


SOFTEN = 0.5


def extended_2(cells, sides, width):
    for axis, dim in sides:
        count = lax.axis_size(axis)
        head = lax.slice_in_dim(cells, 0, width, axis=dim)
        tail = lax.slice_in_dim(cells, cells.shape[dim] - width, cells.shape[dim], axis=dim)
        cells = jnp.concatenate(
            [
                lax.ppermute(tail, axis, [(i, (i + 1) % count) for i in range(count)]),
                cells,
                lax.ppermute(head, axis, [((i + 1) % count, i) for i in range(count)]),
            ],
            axis=dim,
        )
    return cells


def channel_list():
    listed = []
    for pow_z in range(2):
        for pow_x in range(6 - pow_z):
            for pow_y in range(6 - pow_z - pow_x):
                listed.append((pow_x, pow_y, pow_z))
    return listed


def powers(values, highest):
    result = [jnp.ones_like(values)]
    for degree in range(highest):
        result.append(result[-1] * values)
    return result


def contract(form, left, right):
    return jnp.einsum(
        form, left, right, precision=lax.Precision.HIGHEST, preferred_element_type=jnp.float32
    )


def dft_tables(length):
    counter = jnp.arange(length, dtype=jnp.int32)
    product = counter[:, None] * counter[None, :] % length
    angle = product.astype(jnp.float32) * (2.0 * math.pi / length)
    return (jnp.cos(angle), jnp.sin(angle))


def far_accel(local_field, along_x, along_y, along_z):
    accel = [jnp.zeros_like(along_x[1]) for axis_index in range(3)]
    for chan_index, (pow_x, pow_y, pow_z) in enumerate(channel_list()):
        coefficient = local_field[chan_index][:, :, None, :]
        if pow_x > 0:
            accel[0] = accel[0] - coefficient * (
                pow_x * along_x[pow_x - 1] * along_y[pow_y] * along_z[pow_z]
            )
        if pow_y > 0:
            accel[1] = accel[1] - coefficient * (
                pow_y * along_x[pow_x] * along_y[pow_y - 1] * along_z[pow_z]
            )
        if pow_z > 0:
            accel[2] = accel[2] - coefficient * (along_x[pow_x] * along_y[pow_y])
    return jnp.stack(accel)


def y_forward(pieces):
    cos_table, sin_table = dft_tables(pieces.shape[3])
    out_real = contract("cxnz,nk->cxkz", pieces[0], cos_table) + contract(
        "cxnz,nk->cxkz", pieces[1], sin_table
    )
    out_imag = contract("cxnz,nk->cxkz", pieces[1], cos_table) - contract(
        "cxnz,nk->cxkz", pieces[0], sin_table
    )
    return jnp.stack([out_real, out_imag])


def x_forward(pieces):
    cos_table, sin_table = dft_tables(pieces.shape[2])
    out_real = contract("cnyz,nk->cyzk", pieces[0], cos_table) + contract(
        "cnyz,nk->cyzk", pieces[1], sin_table
    )
    out_imag = contract("cnyz,nk->cyzk", pieces[1], cos_table) - contract(
        "cnyz,nk->cyzk", pieces[0], sin_table
    )
    return jnp.stack([out_real, out_imag])


def y_inverse(pieces):
    cos_table, sin_table = dft_tables(pieces.shape[3])
    out_real = contract("cxkz,kn->cxnz", pieces[0], cos_table) - contract(
        "cxkz,kn->cxnz", pieces[1], sin_table
    )
    out_imag = contract("cxkz,kn->cxnz", pieces[1], cos_table) + contract(
        "cxkz,kn->cxnz", pieces[0], sin_table
    )
    return jnp.stack([out_real, out_imag])


def z_inverse(pieces):
    cos_table, sin_table = dft_tables(pieces.shape[4])
    out_real = contract("cxyk,kn->cxyn", pieces[0], cos_table) - contract(
        "cxyk,kn->cxyn", pieces[1], sin_table
    )
    out_imag = contract("cxyk,kn->cxyn", pieces[1], cos_table) + contract(
        "cxyk,kn->cxyn", pieces[0], sin_table
    )
    return jnp.stack([out_real, out_imag])


def inverse_pass(local_real, local_imag, total_x):
    chan_count = local_real.shape[0]
    rows_k = local_real.shape[1]
    planes_k = local_real.shape[2] // total_x
    spec_real = local_real.reshape(chan_count, rows_k, planes_k, total_x)
    spec_imag = local_imag.reshape(chan_count, rows_k, planes_k, total_x)
    cos_table, sin_table = dft_tables(total_x)
    along_real = contract("cyzk,kn->cnyz", spec_real, cos_table) - contract(
        "cyzk,kn->cnyz", spec_imag, sin_table
    )
    along_imag = contract("cyzk,kn->cnyz", spec_imag, cos_table) + contract(
        "cyzk,kn->cnyz", spec_real, sin_table
    )
    stacked = jnp.stack([along_real, along_imag])
    lines_y = y_inverse(lax.all_to_all(stacked, "gx", split_axis=2, concat_axis=3, tiled=True))
    return z_inverse(lax.all_to_all(lines_y, "gy", split_axis=3, concat_axis=4, tiled=True))


def far_field(offsets, masses, kernel):
    planes_x = offsets.shape[1]
    rows_y = offsets.shape[2]
    cells_z = offsets.shape[3] // BODIES
    total_x = planes_x * lax.axis_size("gx")
    total_y = rows_y * lax.axis_size("gy")
    body_pos = offsets.reshape(3, planes_x, rows_y, BODIES, cells_z)
    mass_cells = masses.reshape(planes_x, rows_y, BODIES, cells_z)
    scaled = 2.0 * body_pos - 1.0
    along_x = powers(scaled[0], 5)
    along_y = powers(scaled[1], 5)
    along_z = powers(scaled[2], 1)
    listed = channel_list()
    chan_count = len(listed)
    moments = jnp.stack(
        [
            jnp.sum(mass_cells * (along_x[pow_x] * along_y[pow_y] * along_z[pow_z]), axis=2)
            for pow_x, pow_y, pow_z in listed
        ]
    )
    cos_table, sin_table = dft_tables(cells_z)
    first_real = contract("cxyn,nk->cxyk", moments, cos_table)
    first_imag = -contract("cxyn,nk->cxyk", moments, sin_table)
    stacked = jnp.stack([first_real, first_imag])
    lines_y = y_forward(lax.all_to_all(stacked, "gy", split_axis=4, concat_axis=3, tiled=True))
    spectrum = x_forward(lax.all_to_all(lines_y, "gx", split_axis=3, concat_axis=2, tiled=True))
    rows_k = spectrum.shape[2]
    spec_real = spectrum[0].reshape(chan_count, rows_k, -1)
    spec_imag = spectrum[1].reshape(chan_count, rows_k, -1)
    gain_real = kernel[:, 0]
    gain_imag = kernel[:, 1]
    local_real = contract("dcyk,cyk->dyk", gain_real, spec_real) - contract(
        "dcyk,cyk->dyk", gain_imag, spec_imag
    )
    local_imag = contract("dcyk,cyk->dyk", gain_real, spec_imag) + contract(
        "dcyk,cyk->dyk", gain_imag, spec_real
    )
    inv_count = 1.0 / (total_x * total_y * cells_z)
    paired = inverse_pass(
        local_real[0::2] - local_imag[1::2], local_imag[0::2] + local_real[1::2], total_x
    )
    local_field = (
        jnp.stack([paired[0], paired[1]], axis=1).reshape(chan_count, planes_x, rows_y, cells_z)
        * inv_count
    )
    return far_accel(local_field, along_x, along_y, along_z)


def near_field(offsets, masses):
    planes_x = offsets.shape[1]
    rows_y = offsets.shape[2]
    row_width = offsets.shape[3]
    cells_z = row_width // BODIES
    packed_bodies = jnp.concatenate([offsets, masses[None]], axis=0)
    extended = extended_2(packed_bodies, (("gx", 1), ("gy", 2)), 1)
    own_pos = offsets.reshape(3, planes_x, rows_y, BODIES, cells_z)
    target = jnp.tile(own_pos, (1, 1, 1, 1, BODIES))
    summed = jnp.zeros(target.shape, jnp.float32)
    for shift_x in (-1, 0, 1):
        for shift_y in (-1, 0, 1):
            window_cells = extended[
                :, 1 + shift_x : 1 + shift_x + planes_x, 1 + shift_y : 1 + shift_y + rows_y
            ]
            window_cells = window_cells.reshape(4, planes_x, rows_y, BODIES, cells_z)
            for shift_z in (-1, 0, 1):
                neighbour = jnp.roll(window_cells, -shift_z, axis=4).reshape(
                    4, planes_x, rows_y, 1, row_width
                )
                offset_vec = jnp.array([shift_x, shift_y, shift_z], jnp.float32).reshape(
                    3, 1, 1, 1, 1
                )
                separation = neighbour[:3] + offset_vec - target
                distance_sq = jnp.sum(separation * separation, axis=0) + SOFTEN * SOFTEN
                inverse_r = lax.rsqrt(distance_sq)
                summed = summed + separation * (neighbour[3] * inverse_r * inverse_r * inverse_r)
    summed = summed.reshape(3, planes_x, rows_y, BODIES, BODIES, cells_z).sum(axis=4)
    return summed


def local(offsets, masses, kernel):
    planes_x = offsets.shape[1]
    rows_y = offsets.shape[2]
    row_width = offsets.shape[3]
    far_part = far_field(offsets, masses, kernel)
    near_part = near_field(offsets, masses)
    return (far_part + near_part).reshape(3, planes_x, rows_y, row_width)


def solution(mesh):
    placed = (P(None, "gx", "gy", None), P("gx", "gy", None), P(None, None, None, "gx", "gy"))
    return jax.shard_map(
        local, mesh=mesh, in_specs=placed, out_specs=P(None, "gx", "gy", None), check_vma=False
    )
```

profile of v0, /device:TPU:0, one launch (start us, length us, event | category | flops | bytes accessed | tf_op | source)
XLA Modules:
  0.0 144.1 jit_solution(11666281279524905123)
XLA Ops:
  0.0 1.5 %pad_maximum_fusion.6 = f32[4,1,8,512]{3,2,1,0:T(8,128)} fusion(f32[1,1,8,512]{3,2,1,0:T(8,128)} %bitcast.705, f32[3,1,8,512]{3,2,1,0:T(8,128)} %param.30), kind=kLoop, calls=%fused_computation.219 | loop fusion | flops 16384 | bytes 131072 | tf_op jit(solution)/shard_map/concatenate | solution.py:191
  1.5 5.4 %collective-permute-start.1 = (f32[4,1,8,512]{3,2,1,0:T(8,128)}, f32[4,1,8,512]{3,2,1,0:T(8,128)S(1)}, u32[]{:S(2)}, u32[]{:S(2)}) collective-permute-start(f32[4,1,8,512]{3,2,1,0:T(8,128)} %pad_maximum_fusion.6), channel_id=1, source_target_pairs={{2,0},{4,2},{6,4},{8,6},{10,8},{12,10},{14,12},{16,14},{18,16},{20... | collective-permute-start | bytes 196616 | tf_op jit(solution)/shard_map/ppermute | solution.py:23
  11.0 1.1 copy.171
  12.1 2.3 %reshape.4056 = f32[2,1,18432]{2,1,0:T(1,128)} reshape(f32[64,2,1,8,36]{4,3,2,1,0:T(8,128)} %bitcast.702) | data formatting | bytes 294912
  14.4 3.4 %all-to-all-start = ((f32[2,1,18432]{2,1,0:T(1,128)}), f32[2,1,18432]{2,1,0:T(1,128)S(1)}, u32[]{:S(2)}, u32[]{:S(2)}) async-start(f32[2,1,18432]{2,1,0:T(1,128)} %reshape.4056), calls=%async_computation | async-start | bytes 294912 | tf_op jit(solution)/shard_map/all_to_all | solution.py:162
  19.0 6.0 %fusion.412 = (bf16[36,1,36,1,512]{4,1,3,2,0:T(2,128)(2,1)}, bf16[36,1,36,1,512]{4,1,3,2,0:T(2,128)(2,1)}) fusion(bf16[36,2,36,1,512]{4,1,3,2,0:T(2,128)(2,1)S(1)} %copy-done), kind=kLoop, calls=%fused_computation.657 | loop fusion | bytes 5308416 | tf_op jit(solution)/shard_map/slice | solution.py:168
  26.5 2.1 %collective-permute-start.3 = (f32[4,3,1,512]{3,2,1,0:T(1,128)S(1)}, f32[4,3,1,512]{3,2,1,0:T(1,128)S(1)}, u32[]{:S(2)}, u32[]{:S(2)}) collective-permute-start(f32[4,3,1,512]{3,2,1,0:T(1,128)S(1)} %get-tuple-element.103), channel_id=1, source_target_pairs={{1,0},{0,1},{3,2},{2,3},{5,4},{4,5},{7,6},{6,7},{9,8},{8,9},{11,10... | collective-permute-start | bytes 73736 | tf_op jit(solution)/shard_map/ppermute | solution.py:23
  32.3 1.1 reduce.99
  37.1 1.2 reshape.4058
  38.3 5.5 %all-to-all-start.1 = ((f32[16,1,2304]{2,1,0:T(1,128)}), f32[16,1,2304]{2,1,0:T(1,128)}, u32[]{:S(2)}, u32[]{:S(2)}) async-start(f32[16,1,2304]{2,1,0:T(1,128)} %reshape.4058), calls=%async_computation.1 | async-start | bytes 294912 | tf_op jit(solution)/shard_map/all_to_all | solution.py:163
  54.1 1.4 pad_maximum_fusion.8
  55.5 1.5 %slice.732 = f32[3,8,8,64]{3,2,1,0:T(8,128)} reshape(f32[3,1,8,512]{3,2,1,0:T(8,128)} %get-tuple-element.99) | data formatting | bytes 98304 | tf_op jit(solution)/shard_map/slice | solution.py:209
  57.0 1.5 %slice.759 = f32[3,8,8,64]{3,2,1,0:T(8,128)} reshape(f32[3,1,8,512]{3,2,1,0:T(8,128)} %get-tuple-element.100) | data formatting | bytes 98304 | tf_op jit(solution)/shard_map/slice | solution.py:209
  60.9 0.9 slice.680
  61.8 1.5 %slice.652 = f32[3,8,8,64]{3,2,1,0:T(8,128)} reshape(f32[3,1,8,512]{3,2,1,0:T(8,128)} %get-tuple-element.208) | data formatting | bytes 98304 | tf_op jit(solution)/shard_map/slice | solution.py:209
  71.5 2.9 %multiply_reduce_fusion.26 = (f32[8,8,8,64]{3,2,1,0:T(8,128)S(1)}, f32[8,8,8,64]{3,2,1,0:T(8,128)S(1)}, f32[8,8,8,64]{3,2,1,0:T(8,128)S(1)}, f32[8,8,8,64]{3,2,1...) fusion(f32[3,8,8,64]{3,2,1,0:T(8,128)S(1)} %tile.10, ...), kind=kLoop, calls=%fused_computation.54 | loop fusion | flops 4980736 | bytes 3424256 | tf_op jit(solution)/shard_map/reduce_sum | solution.py:210
  75.5 1.0 multiply_reduce_fusion.25
  96.3 2.7 %reduce.100 = f32[16,2304]{1,0:T(8,128)} reduce(f32[16,1,2304]{2,1,0:T(1,128)} %all-to-all-done.1, f32[]{:T(128)} %broadcast.2241), dimensions={1}, to_apply=%all_to_all.19.reduce_sub_computation | reduce | bytes 294916 | tf_op jit(solution)/shard_map/all_to_all | solution.py:163
  99.0 1.5 %reshape.4059 = f32[16,2,1,32,36]{4,3,2,1,0:T(8,128)S(1)} reshape(f32[16,2304]{1,0:T(8,128)} %reduce.100) | data formatting | bytes 294912
  103.0 4.1 %fusion = (f32[512,36]{0,1:T(8,128)S(1)}, f32[512,36]{0,1:T(8,128)S(1)}, f32[512,36]{0,1:T(8,128)S(1)}, f32[512,36]{0,1:T(8,128)S(1)}) fusion(f32[512,36]{0,1:T(8,128)S(1)} %copy.270, bf16[36,1,36,1,512]{4,1,3,2,0:T(2,128)(2,1)} %get-tuple-element.74, f32[512,36]{0,1:T(8,128)S(1)} %copy.271, bf16[36,1,36,1,512]{4,1,3,2,0:T(2,128)(2,1)S(1)} %copy-done.1), kind=kLoop, calls=%fused_computation.4 | loop fusion | flops 6561792 | bytes 3096576 | tf_op jit(solution)/shard_map/dcyk,cyk->dyk/dot_general | solution.py:47
  107.5 1.3 fusion.286
  108.9 1.3 fusion.284
  110.1 1.3 fusion.10
  111.4 1.3 fusion.9
  113.1 0.9 reshape.4060
  114.0 5.8 %all-to-all-start.2 = ((f32[16,1,1152]{2,1,0:T(1,128)}), f32[16,1,1152]{2,1,0:T(1,128)S(1)}, u32[]{:S(2)}, u32[]{:S(2)}) async-start(f32[16,1,1152]{2,1,0:T(1,128)} %reshape.4060), calls=%async_computation.2 | async-start | bytes 147456 | tf_op jit(solution)/shard_map/all_to_all | solution.py:134
  119.8 1.7 %multiply_multiply_fusion.7 = f32[8,8,8,64]{3,2,1,0:T(8,128)} fusion(f32[8,8,8,64]{3,2,1,0:T(8,128)} %get-tuple-element.63, f32[8,8,64]{2,1,0:T(8,128)S(1)} %copy-done.64), kind=kLoop, calls=%fused_computation.65 | loop fusion | flops 131072 | bytes 278528 | tf_op jit(solution)/shard_map/mul | solution.py:212
  121.5 5.3 %all-to-all-done.2 = f32[16,1,1152]{2,1,0:T(1,128)S(1)} async-done(((f32[16,1,1152]{2,1,0:T(1,128)}), f32[16,1,1152]{2,1,0:T(1,128)S(1)}, u32[]{:S(2)}, u32[]{:S(2)}) %all-to-all-start.2) | async-done | bytes 73760 | tf_op jit(solution)/shard_map/all_to_all | solution.py:134
  129.8 0.9 reshape.4062
  130.7 3.3 %all-to-all-start.3 = ((f32[2,1,9216]{2,1,0:T(1,128)}), f32[2,1,9216]{2,1,0:T(1,128)S(1)}, u32[]{:S(2)}, u32[]{:S(2)}) async-start(f32[2,1,9216]{2,1,0:T(1,128)} %reshape.4062), calls=%async_computation.3 | async-start | bytes 147456 | tf_op jit(solution)/shard_map/all_to_all | solution.py:135
  134.2 5.3 %add_reduce_fusion = f32[3,8,8,64]{3,2,1,0:T(8,128)S(1)} fusion(f32[8,8,8,64]{3,2,1,0:T(8,128)S(1)} %copy-done.12, f32[3,8,8,64]{3,2,1,0:T(8,128)} %copy-done.15, f32[8,8,8,64]{3,2,1,0:T(8,128)S(1)} %copy-done.11, f32[3,8,8,64]{3,2,1,0:T(8,128)} %copy-done.18, f32[8,8,8,64]{3,2,1,0:T(8,128)S(1)} %copy-done.10, f32[3,8,8,64]{3,2,1,0:T(8,128)} %copy-done.17, ...), kind=kLoop, calls=%fused_computation.27 | loop fusion | flops 7950336 | bytes 4915200 | tf_op jit(solution)/shard_map/reduce_sum | solution.py:213
  139.6 0.9 reduce.102
  (354 shorter events, 64.4 us)
Async XLA Ops:
  0.0 17.9 %copy-start.2 = (f32[3,1,8,512]{3,2,1,0:T(8,128)S(1)}, f32[3,1,8,512]{3,2,1,0:T(8,128)}, u32[]{:S(2)}) copy-start(f32[3,1,8,512]{3,2,1,0:T(8,128)} %param.30) | copy-start | bytes 147460
  0.0 17.8 %copy-start.3 = (f32[1,8,512]{2,1,0:T(8,128)S(1)}, f32[1,8,512]{2,1,0:T(8,128)}, u32[]{:S(2)}) copy-start(f32[1,8,512]{2,1,0:T(8,128)} %param.31) | copy-start | bytes 49156
  1.5 24.3 %collective-permute-start.1 = (f32[4,1,8,512]{3,2,1,0:T(8,128)}, f32[4,1,8,512]{3,2,1,0:T(8,128)S(1)}, u32[]{:S(2)}, u32[]{:S(2)}) collective-permute-start(f32[4,1,8,512]{3,2,1,0:T(8,128)} %pad_maximum_fusion.6), channel_id=1, source_target_pairs={{2,0},{4,2},{6,4},{8,6},{10,8},{12,10},{14,12},{16,14},{18,16},{20... | collective-permute-start | bytes 196616 | tf_op jit(solution)/shard_map/ppermute | solution.py:23
  6.9 19.2 %collective-permute-start = (f32[4,1,8,512]{3,2,1,0:T(8,128)}, f32[4,1,8,512]{3,2,1,0:T(8,128)S(1)}, u32[]{:S(2)}, u32[]{:S(2)}) collective-permute-start(f32[4,1,8,512]{3,2,1,0:T(8,128)} %pad_maximum_fusion.6), channel_id=1, source_target_pairs={{0,2},{2,4},{4,6},{6,8},{8,10},{10,12},{12,14},{14,16},{16,18},{18... | collective-permute-start | bytes 196616 | tf_op jit(solution)/shard_map/ppermute | solution.py:21
  7.7 10.1 %copy-start.45 = (f32[8,8,64]{2,1,0:T(8,128)}, f32[8,8,64]{2,1,0:T(8,128)S(1)}, u32[]{:S(2)}) copy-start(f32[8,8,64]{2,1,0:T(8,128)S(1)} %reshape.4014) | copy-start | bytes 49156
  9.4 9.5 %copy-start = (bf16[36,2,36,1,512]{4,1,3,2,0:T(2,128)(2,1)S(1)}, bf16[36,2,36,1,512]{4,1,3,2,0:T(2,128)(2,1)}, u32[]{:S(2)}) copy-start(bf16[36,2,36,1,512]{4,1,3,2,0:T(2,128)(2,1)} %param.32) | copy-start | bytes 7962628
  14.4 17.3 %all-to-all-start = ((f32[2,1,18432]{2,1,0:T(1,128)}), f32[2,1,18432]{2,1,0:T(1,128)S(1)}, u32[]{:S(2)}, u32[]{:S(2)}) async-start(f32[2,1,18432]{2,1,0:T(1,128)} %reshape.4056), calls=%async_computation | async-start | bytes 294912 | tf_op jit(solution)/shard_map/all_to_all | solution.py:162
  25.1 46.1 %copy-start.36 = (f32[3,8,8,64]{3,2,1,0:T(8,128)}, f32[3,8,8,64]{3,2,1,0:T(8,128)S(1)}, u32[]{:S(2)}) copy-start(f32[3,8,8,64]{3,2,1,0:T(8,128)S(1)} %get-tuple-element.223) | copy-start | bytes 147460
  25.2 46.1 %copy-start.37 = (f32[3,8,8,64]{3,2,1,0:T(8,128)}, f32[3,8,8,64]{3,2,1,0:T(8,128)S(1)}, u32[]{:S(2)}) copy-start(f32[3,8,8,64]{3,2,1,0:T(8,128)S(1)} %get-tuple-element.224) | copy-start | bytes 147460
  26.5 17.3 %collective-permute-start.3 = (f32[4,3,1,512]{3,2,1,0:T(1,128)S(1)}, f32[4,3,1,512]{3,2,1,0:T(1,128)S(1)}, u32[]{:S(2)}, u32[]{:S(2)}) collective-permute-start(f32[4,3,1,512]{3,2,1,0:T(1,128)S(1)} %get-tuple-element.103), channel_id=1, source_target_pairs={{1,0},{0,1},{3,2},{2,3},{5,4},{4,5},{7,6},{6,7},{9,8},{8,9},{11,10... | collective-permute-start | bytes 73736 | tf_op jit(solution)/shard_map/ppermute | solution.py:23
  28.5 15.3 %collective-permute-start.2 = (f32[4,3,1,512]{3,2,1,0:T(1,128)S(1)}, f32[4,3,1,512]{3,2,1,0:T(1,128)S(1)}, u32[]{:S(2)}, u32[]{:S(2)}) collective-permute-start(f32[4,3,1,512]{3,2,1,0:T(1,128)S(1)} %get-tuple-element.104), channel_id=1, source_target_pairs={{0,1},{1,0},{2,3},{3,2},{4,5},{5,4},{6,7},{7,6},{8,9},{9,8},{10,11... | collective-permute-start | bytes 73736 | tf_op jit(solution)/shard_map/ppermute | solution.py:21
  38.3 58.0 %all-to-all-start.1 = ((f32[16,1,2304]{2,1,0:T(1,128)}), f32[16,1,2304]{2,1,0:T(1,128)}, u32[]{:S(2)}, u32[]{:S(2)}) async-start(f32[16,1,2304]{2,1,0:T(1,128)} %reshape.4058), calls=%async_computation.1 | async-start | bytes 294912 | tf_op jit(solution)/shard_map/all_to_all | solution.py:163
  46.3 25.0 %copy-start.25 = (f32[3,8,8,64]{3,2,1,0:T(8,128)}, f32[3,8,8,64]{3,2,1,0:T(8,128)S(1)}, u32[]{:S(2)}) copy-start(f32[3,8,8,64]{3,2,1,0:T(8,128)S(1)} %fusion.85) | copy-start | bytes 147460
  47.7 27.8 %copy-start.15 = (f32[3,8,8,64]{3,2,1,0:T(8,128)}, f32[3,8,8,64]{3,2,1,0:T(8,128)S(1)}, u32[]{:S(2)}) copy-start(f32[3,8,8,64]{3,2,1,0:T(8,128)S(1)} %fusion.37) | copy-start | bytes 147460
  60.9 9.5 %copy-start.75 = (f32[3]{0:T(128)S(1)}, f32[3]{0:T(128)}, u32[]{:S(2)}) copy-start(f32[3]{0:T(128)} %constant.135.clone) | copy-start | bytes 40
  66.8 8.6 %copy-start.16 = (f32[3,8,8,64]{3,2,1,0:T(8,128)}, f32[3,8,8,64]{3,2,1,0:T(8,128)S(1)}, u32[]{:S(2)}) copy-start(f32[3,8,8,64]{3,2,1,0:T(8,128)S(1)} %fusion.49) | copy-start | bytes 147460
  84.9 6.8 %copy-start.49 = (f32[8,8,64]{2,1,0:T(8,128)S(1)}, f32[8,8,64]{2,1,0:T(8,128)}, u32[]{:S(2)}) copy-start(f32[8,8,64]{2,1,0:T(8,128)} %maximum_bitcast_fusion) | copy-start | bytes 49156
  86.4 6.9 %copy-start.57 = (f32[8,8,64]{2,1,0:T(8,128)S(1)}, f32[8,8,64]{2,1,0:T(8,128)}, u32[]{:S(2)}) copy-start(f32[8,8,64]{2,1,0:T(8,128)} %mul.4736) | copy-start | bytes 49156
  107.2 12.6 %copy-start.64 = (f32[8,8,64]{2,1,0:T(8,128)S(1)}, f32[8,8,64]{2,1,0:T(8,128)}, u32[]{:S(2)}) copy-start(f32[8,8,64]{2,1,0:T(8,128)} %mul.4760) | copy-start | bytes 49156
  113.0 21.1 %copy-start.4 = (f32[8,8,8,64]{3,2,1,0:T(8,128)S(1)}, f32[8,8,8,64]{3,2,1,0:T(8,128)}, u32[]{:S(2)}) copy-start(f32[8,8,8,64]{3,2,1,0:T(8,128)} %multiply_multiply_fusion.13) | copy-start | bytes 393220
  113.0 21.1 %copy-start.5 = (f32[8,8,8,64]{3,2,1,0:T(8,128)S(1)}, f32[8,8,8,64]{3,2,1,0:T(8,128)}, u32[]{:S(2)}) copy-start(f32[8,8,8,64]{3,2,1,0:T(8,128)} %multiply_multiply_fusion.25) | copy-start | bytes 393220
  113.0 21.1 %copy-start.6 = (f32[8,8,8,64]{3,2,1,0:T(8,128)S(1)}, f32[8,8,8,64]{3,2,1,0:T(8,128)}, u32[]{:S(2)}) copy-start(f32[8,8,8,64]{3,2,1,0:T(8,128)} %multiply_multiply_fusion.6) | copy-start | bytes 393220
  113.0 21.1 %copy-start.7 = (f32[8,8,8,64]{3,2,1,0:T(8,128)S(1)}, f32[8,8,8,64]{3,2,1,0:T(8,128)}, u32[]{:S(2)}) copy-start(f32[8,8,8,64]{3,2,1,0:T(8,128)} %multiply_multiply_fusion.5) | copy-start | bytes 393220
  113.0 21.1 %copy-start.8 = (f32[8,8,8,64]{3,2,1,0:T(8,128)S(1)}, f32[8,8,8,64]{3,2,1,0:T(8,128)}, u32[]{:S(2)}) copy-start(f32[8,8,8,64]{3,2,1,0:T(8,128)} %multiply_multiply_fusion.4) | copy-start | bytes 393220
  113.0 21.1 %copy-start.9 = (f32[8,8,8,64]{3,2,1,0:T(8,128)S(1)}, f32[8,8,8,64]{3,2,1,0:T(8,128)}, u32[]{:S(2)}) copy-start(f32[8,8,8,64]{3,2,1,0:T(8,128)} %multiply_multiply_fusion.3) | copy-start | bytes 393220
  113.0 21.1 %copy-start.10 = (f32[8,8,8,64]{3,2,1,0:T(8,128)S(1)}, f32[8,8,8,64]{3,2,1,0:T(8,128)}, u32[]{:S(2)}) copy-start(f32[8,8,8,64]{3,2,1,0:T(8,128)} %multiply_multiply_fusion.2) | copy-start | bytes 393220
  113.1 21.1 %copy-start.11 = (f32[8,8,8,64]{3,2,1,0:T(8,128)S(1)}, f32[8,8,8,64]{3,2,1,0:T(8,128)}, u32[]{:S(2)}) copy-start(f32[8,8,8,64]{3,2,1,0:T(8,128)} %multiply_multiply_fusion.1) | copy-start | bytes 393220
  113.1 21.1 %copy-start.12 = (f32[8,8,8,64]{3,2,1,0:T(8,128)S(1)}, f32[8,8,8,64]{3,2,1,0:T(8,128)}, u32[]{:S(2)}) copy-start(f32[8,8,8,64]{3,2,1,0:T(8,128)} %multiply_multiply_fusion) | copy-start | bytes 393220
  113.1 21.1 %copy-start.13 = (f32[8,8,8,64]{3,2,1,0:T(8,128)S(1)}, f32[8,8,8,64]{3,2,1,0:T(8,128)}, u32[]{:S(2)}) copy-start(f32[8,8,8,64]{3,2,1,0:T(8,128)} %multiply_multiply_fusion.26) | copy-start | bytes 393220
  113.1 21.1 %copy-start.14 = (f32[8,8,8,64]{3,2,1,0:T(8,128)S(1)}, f32[8,8,8,64]{3,2,1,0:T(8,128)}, u32[]{:S(2)}) copy-start(f32[8,8,8,64]{3,2,1,0:T(8,128)} %multiply_multiply_fusion.24) | copy-start | bytes 393220
  114.0 12.8 %all-to-all-start.2 = ((f32[16,1,1152]{2,1,0:T(1,128)}), f32[16,1,1152]{2,1,0:T(1,128)S(1)}, u32[]{:S(2)}, u32[]{:S(2)}) async-start(f32[16,1,1152]{2,1,0:T(1,128)} %reshape.4060), calls=%async_computation.2 | async-start | bytes 147456 | tf_op jit(solution)/shard_map/all_to_all | solution.py:134
  130.7 8.9 %all-to-all-start.3 = ((f32[2,1,9216]{2,1,0:T(1,128)}), f32[2,1,9216]{2,1,0:T(1,128)S(1)}, u32[]{:S(2)}, u32[]{:S(2)}) async-start(f32[2,1,9216]{2,1,0:T(1,128)} %reshape.4062), calls=%async_computation.3 | async-start | bytes 147456 | tf_op jit(solution)/shard_map/all_to_all | solution.py:135
  (58 other events, 276.5 us)
where the time goes:
time: 146 us; the launch traced here: 144 us
  other arithmetic  59.7 us (41%)
  local copies, waits for them, and re-layouts  39.3 us (27%)
  starting transfers between devices  25.5 us (17%)
  matrix products  12.4 us (8%)
  waiting for transfers between devices  5.33 us (4%)
  between operations  1.76 us (1%)
    mul x43, other arithmetic, near_field(): neighbour[3] * inverse_r * inverse_r * inverse_r  26.3 us
    dot_general x22, matrix products, contract(): jnp.einsum(form, left, right, precision=lax.Precision.HIGHEST, preferred_...  12.4 us
    slice x9, local copies, waits for them, and re-layouts, near_field(): separation = neighbour[:3] + offset_vec - target  9.29 us
    unnamed x174, local copies, waits for them, and re-layouts  8.68 us
    add x21, other arithmetic, near_field(): separation = neighbour[:3] + offset_vec - target  8.11 us
    ppermute x2, starting transfers between devices, extended_2(): lax.ppermute(head, axis, [((i + 1) % count, i) for i in range(count)])  7.47 us
    slice x1, local copies, waits for them, and re-layouts, far_field(): gain_imag = kernel[:, 1]  5.99 us
    all_to_all x1, starting transfers between devices, inverse_pass(): lax.all_to_all(stacked, 'gx', split_axis=2, concat_axis=3, tiled=True)  5.78 us
  transfers between devices with their start and end apart: 8, of which 1 were waited for; matrix products, arithmetic and copies ran while one was open for 58% of the time, Pallas kernels for 0%

commit v1 on v0

v1 whole, which is shorter than its diff:
```python
import functools
import math

import jax
import jax.numpy as jnp
import numpy as np
from jax import lax
from jax.experimental import pallas as pl
from jax.experimental.pallas import tpu as pltpu
from jax.sharding import PartitionSpec as P

BODIES = 8
SOFTEN = 0.5
LANES = 128
MESH = pl.DeviceIdType.MESH
HIGHEST = lax.Precision.HIGHEST


def channel_list():
    listed = []
    for pow_z in range(2):
        for pow_x in range(6 - pow_z):
            for pow_y in range(6 - pow_z - pow_x):
                listed.append((pow_x, pow_y, pow_z))
    return listed


CHANNELS = channel_list()
COUNT = len(CHANNELS)
HALF = COUNT // 2


class Sizes:
    def __init__(self, n_gx, n_gy, planes_x, rows_y, row_width, waves):
        self.n_gx, self.n_gy = n_gx, n_gy
        self.rows_y = rows_y
        self.cells_z = row_width // BODIES
        self.width = row_width
        self.total_x = planes_x * n_gx
        self.total_y = rows_y * n_gy
        self.kzw = self.cells_z // n_gy
        self.q = LANES // (2 * self.kzw)
        self.groups = waves // LANES
        self.wg = LANES // self.total_x
        self.rows = -(-COUNT // self.q)
        self.rows_pad = -(-self.rows // 8) * 8
        self.prow = -(-HALF // self.q)
        self.prow_pad = -(-self.prow // 8) * 8
        assert planes_x == 1 and self.total_y == n_gx and rows_y == 8
        assert 2 * self.cells_z == LANES and self.q % 2 == 0
        assert 2 * self.q * self.groups == self.total_x


def angle(left, right, length):
    return (np.multiply.outer(left, right) % length) * (2.0 * math.pi / length)


def tables(z):
    cells, kzw, q, wg, nx = z.cells_z, z.kzw, z.q, z.wg, z.total_x
    zf = np.zeros((z.n_gy, q // 2, 2, cells, 2, q, kzw))
    for h in range(z.n_gy):
        ang = angle(np.arange(cells), h * kzw + np.arange(kzw), cells)
        for u in range(q // 2):
            for b in range(2):
                zf[h, u, b, :, 0, 2 * u + b] = np.cos(ang)
                zf[h, u, b, :, 1, 2 * u + b] = -np.sin(ang)
    zf = zf.reshape(z.n_gy, q // 2, LANES, LANES)
    ang = angle(np.arange(nx), np.arange(nx), nx)
    c, s = np.cos(ang), np.sin(ang)
    xf = np.zeros((2, nx, wg, 2, wg, nx))
    xi = np.zeros((2, wg, nx, 2, nx, wg))
    for k in range(wg):
        xf[0, :, k, 0, k], xf[1, :, k, 0, k] = c, s
        xf[0, :, k, 1, k], xf[1, :, k, 1, k] = -s, c
        xi[0, k, :, 0, :, k], xi[1, k, :, 0, :, k] = c, -s
        xi[0, k, :, 1, :, k], xi[1, k, :, 1, :, k] = s, c
    xf = xf.reshape(2 * LANES, 2 * LANES)
    xi = xi.reshape(2 * LANES, 2 * LANES)
    zi = np.zeros((z.n_gy, 2, q, kzw, q, 2, 2, cells))
    scale = 1.0 / (z.total_x * z.total_y * cells)
    for h in range(z.n_gy):
        ang = angle(h * kzw + np.arange(kzw), np.arange(cells), cells)
        c, s = np.cos(ang) * scale, np.sin(ang) * scale
        for i in range(q):
            for copy in range(2):
                zi[h, 0, i, :, i, 0, copy], zi[h, 1, i, :, i, 0, copy] = c, -s
                zi[h, 0, i, :, i, 1, copy], zi[h, 1, i, :, i, 1, copy] = s, c
    zi = zi.reshape(z.n_gy, LANES, q * 2 * LANES)
    return [np.asarray(t, np.float32) for t in (zf, xf, xi, zi)]


def dot(left, right):
    return jnp.dot(left, right, precision=HIGHEST, preferred_element_type=jnp.float32)


def times_i(value, sign):
    return pltpu.roll(value, LANES // 2, 1) * sign


def transform(values, direction, sign):
    count = len(values)
    if count == 1:
        return values
    even = transform(values[0::2], direction, sign)
    odd = transform(values[1::2], direction, sign)
    low, high = [], []
    for k in range(count // 2):
        value = odd[k]
        if k * 4 == count:
            value = times_i(value, sign * direction)
        elif k:
            theta = direction * 2.0 * math.pi * k / count
            value = value * math.cos(theta) + times_i(value, sign * math.sin(theta))
        low.append(even[k] + value)
        high.append(even[k] - value)
    return low + high


def exchange(values, lane, chunk):
    count = len(values)
    values = list(values)
    bit = 1
    while bit < count:
        keep = (lane // (chunk * bit)) % 2 == 0
        for i in range(count):
            if i & bit == 0:
                a, b = values[i], values[i | bit]
                values[i] = jnp.where(keep, a, pltpu.roll(b, chunk * bit, 1))
                values[i | bit] = jnp.where(keep, pltpu.roll(a, LANES - chunk * bit, 1), b)
        bit *= 2
    return values


def lane_tiles(value):
    return [value[:, i : i + LANES] for i in range(0, value.shape[1], LANES)]


def powers(value, highest):
    result = [None, value]
    for _ in range(highest - 1):
        result.append(result[-1] * value)
    return result


def scaled_mul(value, power):
    return value if power is None else value * power


def kernel_body(
    z, off_hbm, mass_hbm, gain_hbm, zf_hbm, xf_hbm, xi_hbm, zi_hbm, out_ref,
    off_ref, mass_ref, gain, zf, xf, xi, zi, yb, edge, xh, xc, near_src, acc_ref, mom, msg_b, got_b, spec, coef,
    msg_c, got_c, lines, field,
    load_sem, ysend, yrecv, hsend, hrecv, csend, crecv, bsend, brecv, fsend, frecv,
):
    nx, ny = z.n_gx, z.n_gy
    mx, my = lax.axis_index("gx"), lax.axis_index("gy")
    me = mx * ny + my
    total = nx * ny

    def peer(k):
        other = lax.rem(me + k, total)
        return other // ny, lax.rem(other, ny)

    barrier = pltpu.get_barrier_semaphore()

    def greet(k, carry):
        px, py = peer(k)
        pl.semaphore_signal(barrier, inc=1, device_id=(px, py), device_id_type=MESH)
        return carry

    loads = [
        pltpu.make_async_copy(src, dst, load_sem.at[i])
        for i, (src, dst) in enumerate(
            [(off_hbm, off_ref), (mass_hbm, mass_ref), (zf_hbm.at[my], zf), (xf_hbm, xf), (xi_hbm, xi),
             (zi_hbm, zi), (gain_hbm, gain)]
        )
    ]
    for load in loads:
        load.start()
    lax.fori_loop(1, total, greet, 0)
    loads[0].wait()
    loads[1].wait()

    for comp in range(4):
        value = off_ref[comp] if comp < 3 else mass_ref[...]
        yb[my, comp] = value
        edge[0, comp] = value[0:1]
        edge[1, comp] = value[z.rows_y - 1 : z.rows_y]

    pl.semaphore_wait(barrier, total - 1)

    y_copies = []
    for k in range(1, ny):
        to = lax.rem(my + k, ny)
        copy = pltpu.make_async_remote_copy(
            src_ref=yb.at[my], dst_ref=yb.at[my], send_sem=ysend.at[k], recv_sem=yrecv.at[my],
            device_id=(mx, to), device_id_type=MESH,
        )
        copy.start()
        y_copies.append(copy)
    h_copies = []
    for side in range(2):
        to_x = lax.rem(mx + (1 if side == 0 else nx - 1), nx)
        copy = pltpu.make_async_remote_copy(
            src_ref=yb.at[my], dst_ref=xh.at[side], send_sem=hsend.at[side], recv_sem=hrecv.at[side],
            device_id=(to_x, my), device_id_type=MESH,
        )
        copy.start()
        h_copies.append(copy)
        for end in range(2):
            to_y = lax.rem(my + (1 if end == 0 else ny - 1), ny)
            copy = pltpu.make_async_remote_copy(
                src_ref=edge.at[1 - end], dst_ref=xc.at[side, end], send_sem=csend.at[side, end],
                recv_sem=crecv.at[side, end], device_id=(to_x, to_y), device_id_type=MESH,
            )
            copy.start()
            h_copies.append(copy)

    lane = lax.broadcasted_iota(jnp.int32, (1, LANES), 1)
    first = lane < LANES // 2
    sign = jnp.where(first, -1.0, 1.0).astype(jnp.float32)
    rows, rows_pad = z.rows, z.rows_pad

    if rows_pad != rows:
        mom[...] = jnp.zeros_like(mom)

    def moments_of(block, slot):
        bodies = [yb[block, comp] for comp in range(4)]
        s, t, w = [2.0 * v - 1.0 for v in bodies[:3]]
        along_x, along_y = powers(s, 5), powers(t, 5)
        made = {}
        weighted = bodies[3]
        for e in range(2):
            if e:
                weighted = weighted * w
            for a in range(6 - e):
                partial = scaled_mul(weighted, along_x[a] if a else None)
                for b in range(6 - e - a):
                    tiles = lane_tiles(scaled_mul(partial, along_y[b] if b else None))
                    made[(a, b, e)] = functools.reduce(lambda x, y: x + y, tiles)
        for u in range(z.q // 2):
            for r in range(rows):
                pair = []
                for b in range(2):
                    c = (2 * u + b) * rows + r
                    pair.append(made[CHANNELS[c]] if c < COUNT else jnp.zeros_like(s[:, :LANES]))
                mixed = jnp.where(first, pair[0], pair[1])
                crossed = jnp.where(first, pair[1], pair[0])
                mixed = mixed + pltpu.roll(crossed, LANES // 2, 1)
                mom[u, slot, pl.ds(r, z.rows_y, stride=rows_pad), :] = mixed

    moments_of(my, my)
    for k in range(1, ny):
        source = lax.rem(my + k, ny)
        pltpu.make_async_remote_copy(
            src_ref=yb.at[source], dst_ref=yb.at[source], send_sem=ysend.at[k], recv_sem=yrecv.at[source],
            device_id=(mx, source), device_id_type=MESH,
        ).wait_recv()
        moments_of(source, source)
    loads[2].wait()
    height = ny * z.rows_y * rows_pad
    along = dot(mom[0].reshape(height, LANES), zf[0])
    for u in range(1, z.q // 2):
        along = along + dot(mom[u].reshape(height, LANES), zf[u])
    along = [along[i * rows_pad : (i + 1) * rows_pad] for i in range(z.total_y)]
    for ky, value in enumerate(transform(along, -1.0, sign)):
        msg_b[ky] = value[:rows]

    def send_b(k, carry):
        to = lax.rem(mx + k, nx)
        pltpu.make_async_remote_copy(
            src_ref=msg_b.at[to], dst_ref=got_b.at[mx], send_sem=bsend.at[to], recv_sem=brecv.at[mx],
            device_id=(to, my), device_id_type=MESH,
        ).start()
        return carry

    lax.fori_loop(1, nx, send_b, 0)
    got_b[mx] = msg_b[mx]

    ahead, behind = lax.rem(my + 1, ny), lax.rem(my + ny - 1, ny)

    def fill(dx, main, top, bottom):
        for comp in range(4):
            value = main(comp)
            below = jnp.concatenate([top(comp), value[: z.rows_y - 1]], axis=0)
            above = jnp.concatenate([value[1:], bottom(comp)], axis=0)
            for dy, moved in enumerate((below, value, above)):
                if comp == 0 and dx != 1:
                    moved = moved + (dx - 1.0)
                if comp == 1 and dy != 1:
                    moved = moved + (dy - 1.0)
                for j, tile in enumerate(lane_tiles(moved)):
                    near_src[(dx * 3 + dy) * (z.width // LANES) + j, comp] = tile

    tiles = z.width // LANES

    def near_steps(begin, end):
        target = [[off_ref[comp, :, j * LANES : (j + 1) * LANES] for j in range(tiles)] for comp in range(3)]
        init = tuple(acc_ref[comp, :, j * LANES : (j + 1) * LANES] for comp in range(3) for j in range(tiles))

        def step(index, carry):
            sums = [list(carry[comp * tiles : (comp + 1) * tiles]) for comp in range(3)]
            loaded = [near_src[index, comp] for comp in range(4)]
            turned = [pltpu.roll(v, LANES // 2, 1) for v in loaded]
            for half in range(2):
                both = [
                    jnp.where(first, a, b) if half == 0 else jnp.where(first, b, a)
                    for a, b in zip(loaded, turned)
                ]
                for dz in (-1, 0, 1):
                    src = both if dz == 0 else [pltpu.roll(v, (LANES - dz) % LANES, 1) for v in both]
                    src_z = src[2] + float(dz) if dz else src[2]
                    for j in range(tiles):
                        sx = src[0] - target[0][j]
                        sy = src[1] - target[1][j]
                        sz = src_z - target[2][j]
                        inv = lax.rsqrt(sx * sx + sy * sy + (sz * sz + SOFTEN * SOFTEN))
                        pull = (src[3] * inv) * (inv * inv)
                        sums[0][j] = sums[0][j] + sx * pull
                        sums[1][j] = sums[1][j] + sy * pull
                        sums[2][j] = sums[2][j] + sz * pull
            return tuple(v for comp in sums for v in comp)

        final = lax.fori_loop(begin, end, step, init)
        for comp in range(3):
            for j in range(tiles):
                acc_ref[comp, :, j * LANES : (j + 1) * LANES] = final[comp * tiles + j]

    acc_ref[...] = jnp.zeros_like(acc_ref)
    fill(
        1,
        lambda comp: off_ref[comp] if comp < 3 else mass_ref[...],
        lambda comp: yb[behind, comp, z.rows_y - 1 : z.rows_y],
        lambda comp: yb[ahead, comp, 0:1],
    )
    near_steps(3 * tiles, 6 * tiles)
    for copy in h_copies:
        copy.wait_recv()
    for side in range(2):
        fill(2 * side, lambda comp: xh[side, comp], lambda comp: xc[side, 0, comp], lambda comp: xc[side, 1, comp])
    near_steps(0, 3 * tiles)

    def wait_b(k, carry):
        source = lax.rem(mx + k, nx)
        pltpu.make_async_remote_copy(
            src_ref=msg_b.at[source], dst_ref=got_b.at[source], send_sem=bsend.at[source],
            recv_sem=brecv.at[source], device_id=(source, my), device_id_type=MESH,
        ).wait_recv()
        return carry

    lax.fori_loop(1, nx, wait_b, 0)
    groups, q = z.groups, z.q
    turned = exchange([got_b[i] for i in range(nx)], lane, z.wg)
    loads[3].wait()
    stacked = jnp.concatenate(
        [
            jnp.concatenate([turned[(0 * q + i) * groups + g], turned[(1 * q + i) * groups + g]], axis=1)
            for g in range(groups)
            for i in range(q)
        ],
        axis=0,
    )
    spectrum = dot(stacked, xf[...])
    for g in range(groups):
        part = spectrum[g * q * rows : g * q * rows + COUNT]
        spec[0, g] = part[:, :LANES]
        spec[1, g] = part[:, LANES:]
    loads[6].wait()
    for g in range(groups):
        lanes = slice(g * LANES, (g + 1) * LANES)
        spec_re, spec_im = spec[0, g], spec[1, g]

        def couple(d, carry):
            gain_re = gain[d, 0, :, lanes].astype(jnp.float32)
            gain_im = gain[d, 1, :, lanes].astype(jnp.float32)
            coef[0, g, pl.ds(d, 1), :] = jnp.sum(gain_re * spec_re - gain_im * spec_im, axis=0, keepdims=True)
            coef[1, g, pl.ds(d, 1), :] = jnp.sum(gain_re * spec_im + gain_im * spec_re, axis=0, keepdims=True)
            return carry

        lax.fori_loop(0, COUNT, couple, 0, unroll=6)
    prow = z.prow
    height = q * prow
    pairs = []
    for g in range(groups):
        pair_re = coef[0, g, :HALF] - coef[1, g, HALF:]
        pair_im = coef[1, g, :HALF] + coef[0, g, HALF:]
        pair = jnp.concatenate([pair_re, pair_im], axis=1)
        if height > HALF:
            pair = jnp.concatenate([pair, jnp.zeros((height - HALF, 2 * LANES), jnp.float32)], axis=0)
        pairs.append(pair)
    loads[4].wait()
    back = dot(jnp.concatenate(pairs, axis=0), xi[...])
    ordered = [
        back[g * height + i * prow : g * height + (i + 1) * prow, ri * LANES : (ri + 1) * LANES]
        for ri in range(2)
        for i in range(q)
        for g in range(groups)
    ]
    for x, value in enumerate(exchange(ordered, lane, z.wg)):
        msg_c[x] = value

    def send_c(k, carry):
        px, py = peer(k)
        pltpu.make_async_remote_copy(
            src_ref=msg_c.at[px], dst_ref=got_c.at[my, mx], send_sem=fsend.at[py, px], recv_sem=frecv.at[my, mx],
            device_id=(px, py), device_id_type=MESH,
        ).start()
        return carry

    lax.fori_loop(1, total, send_c, 0)
    got_c[my, mx] = msg_c[mx]

    near_steps(6 * tiles, 9 * tiles)

    def wait_c(k, carry):
        px, py = peer(k)
        pltpu.make_async_remote_copy(
            src_ref=msg_c.at[px], dst_ref=got_c.at[py, px], send_sem=fsend.at[py, px], recv_sem=frecv.at[py, px],
            device_id=(px, py), device_id_type=MESH,
        ).wait_recv()
        return carry

    lax.fori_loop(1, total, wait_c, 0)
    loads[5].wait()
    prow_pad = z.prow_pad
    if prow_pad != prow:
        lines[:, :, prow:, :] = jnp.zeros(lines.shape[:2] + (prow_pad - prow, LANES), jnp.float32)
    result = None
    for h in range(ny):
        for y, value in enumerate(transform([got_c[h, k] for k in range(nx)], 1.0, sign)):
            lines[h, y, :prow] = value
        own = lines[h, pl.ds(my * z.rows_y, z.rows_y)].reshape(z.rows_y * prow_pad, LANES)
        term = dot(own, zi[h])
        result = term if result is None else result + term
    for column, tile in enumerate(lane_tiles(result)):
        field[column] = tile

    def coefficient(c):
        part, p = c // HALF, c % HALF
        i, r = p // prow, p % prow
        return field[i * 2 + part, pl.ds(r, z.rows_y, stride=prow_pad), :]

    number = {channel: c for c, channel in enumerate(CHANNELS)}
    for j in range(tiles):
        lanes = slice(j * LANES, (j + 1) * LANES)
        s, t, w = [2.0 * off_ref[comp, :, lanes] - 1.0 for comp in range(3)]
        along = []
        for e in range(2):
            value = slope_x = slope_y = None
            for b in reversed(range(6 - e)):
                top = 5 - e - b
                inner = coefficient(number[(top, b, e)])
                slope = None
                for a in reversed(range(top)):
                    slope = inner if slope is None else slope * s + inner
                    inner = inner * s + coefficient(number[(a, b, e)])
                slope_y = value if slope_y is None else slope_y * t + value
                value = inner if value is None else value * t + inner
                if slope is not None:
                    slope_x = slope if slope_x is None else slope_x * t + slope
            along.append((value, slope_x, slope_y))
        out_ref[0, :, lanes] = acc_ref[0, :, lanes] - (along[0][1] + w * along[1][1])
        out_ref[1, :, lanes] = acc_ref[1, :, lanes] - (along[0][2] + w * along[1][2])
        out_ref[2, :, lanes] = acc_ref[2, :, lanes] - along[1][0]

    for copy in y_copies:
        copy.wait_send()
    for copy in h_copies:
        copy.wait_send()

    def drain_b(k, carry):
        to = lax.rem(mx + k, nx)
        pltpu.make_async_remote_copy(
            src_ref=msg_b.at[to], dst_ref=got_b.at[mx], send_sem=bsend.at[to], recv_sem=brecv.at[mx],
            device_id=(to, my), device_id_type=MESH,
        ).wait_send()
        return carry

    lax.fori_loop(1, nx, drain_b, 0)

    def drain_c(k, carry):
        px, py = peer(k)
        pltpu.make_async_remote_copy(
            src_ref=msg_c.at[px], dst_ref=got_c.at[my, mx], send_sem=fsend.at[py, px], recv_sem=frecv.at[my, mx],
            device_id=(px, py), device_id_type=MESH,
        ).wait_send()
        return carry

    lax.fori_loop(1, total, drain_c, 0)


def local(offsets, masses, kernel):
    n_gx, n_gy = lax.axis_size("gx"), lax.axis_size("gy")
    _, planes_x, rows_y, width = offsets.shape
    waves = kernel.shape[3] * kernel.shape[4]
    z = Sizes(n_gx, n_gy, planes_x, rows_y, width, waves)
    made = tables(z)
    f32 = jnp.float32
    tiles = width // LANES
    scratch = [
        pltpu.VMEM((3, rows_y, width), f32),
        pltpu.VMEM((rows_y, width), f32),
        pltpu.VMEM((COUNT, 2, COUNT, waves), kernel.dtype),
        pltpu.VMEM(made[0].shape[1:], f32),
        pltpu.VMEM(made[1].shape, f32),
        pltpu.VMEM(made[2].shape, f32),
        pltpu.VMEM(made[3].shape, f32),
        pltpu.VMEM((n_gy, 4, rows_y, width), f32),
        pltpu.VMEM((2, 4, 1, width), f32),
        pltpu.VMEM((2, 4, rows_y, width), f32),
        pltpu.VMEM((2, 2, 4, 1, width), f32),
        pltpu.VMEM((9 * tiles, 4, rows_y, LANES), f32),
        pltpu.VMEM((3, rows_y, width), f32),
        pltpu.VMEM((z.q // 2, n_gy, rows_y * z.rows_pad, LANES), f32),
        pltpu.VMEM((n_gx, z.rows, LANES), f32),
        pltpu.VMEM((n_gx, z.rows, LANES), f32),
        pltpu.VMEM((2, z.groups, COUNT, LANES), f32),
        pltpu.VMEM((2, z.groups, COUNT, LANES), f32),
        pltpu.VMEM((n_gx, z.prow, LANES), f32),
        pltpu.VMEM((n_gy, n_gx, z.prow, LANES), f32),
        pltpu.VMEM((n_gy, n_gx, z.prow_pad, LANES), f32),
        pltpu.VMEM((z.q * 2, rows_y * z.prow_pad, LANES), f32),
        pltpu.SemaphoreType.DMA((7,)),
        pltpu.SemaphoreType.DMA((n_gy,)),
        pltpu.SemaphoreType.DMA((n_gy,)),
        pltpu.SemaphoreType.DMA((2,)),
        pltpu.SemaphoreType.DMA((2,)),
        pltpu.SemaphoreType.DMA((2, 2)),
        pltpu.SemaphoreType.DMA((2, 2)),
        pltpu.SemaphoreType.DMA((n_gx,)),
        pltpu.SemaphoreType.DMA((n_gx,)),
        pltpu.SemaphoreType.DMA((n_gy, n_gx)),
        pltpu.SemaphoreType.DMA((n_gy, n_gx)),
    ]
    out = pl.pallas_call(
        functools.partial(kernel_body, z),
        out_shape=jax.ShapeDtypeStruct((3, rows_y, width), f32),
        in_specs=[pl.BlockSpec(memory_space=pl.ANY)] * 7,
        out_specs=pl.BlockSpec(memory_space=pltpu.VMEM),
        scratch_shapes=scratch,
        compiler_params=pltpu.CompilerParams(
            collective_id=0, has_side_effects=True, vmem_limit_bytes=48 * 1024 * 1024
        ),
    )(
        offsets.reshape(3, rows_y, width), masses.reshape(rows_y, width),
        kernel.reshape(COUNT, 2, COUNT, waves), *[jnp.asarray(t) for t in made],
    )
    return out.reshape(3, planes_x, rows_y, width)


def solution(mesh):
    placed = (P(None, "gx", "gy", None), P("gx", "gy", None), P(None, None, None, "gx", "gy"))
    return jax.shard_map(
        local, mesh=mesh, in_specs=placed, out_specs=P(None, "gx", "gy", None), check_vma=False
    )
```

time: 146 us -> 30.6 us (0.21); the launches traced: 144 us -> 30.5 us
  other arithmetic: 59.7 us -> 0 us
  local copies, waits for them, and re-layouts: 39.3 us -> 3.09 us
  Pallas kernels: 0 us -> 27.3 us
  starting transfers between devices: 25.5 us -> 0 us
  matrix products: 12.4 us -> 0 us
  waiting for transfers between devices: 5.33 us -> 0 us
  between operations: 1.76 us -> 0.08 us
    pallas_call x0 -> x1, Pallas kernels: none -> 27.3 us  [local(): pl.pallas_call(functools.partial(kernel_body, z), out_shape=jax.ShapeDtyp...]
    mul x45 -> x0, other arithmetic: 26.3 us -> none  [the longest x43 26.3 us: near_field(): neighbour[3] * inverse_r * inverse_r * inverse_r]
    all_to_all x4 -> x0, starting transfers between devices: 18 us -> none  [the longest x1 5.78 us: inverse_pass(): lax.all_to_all(stacked, 'gx', split_axis=2, concat_axis=3, tiled=True)]
    slice x37 -> x0, local copies, waits for them, and re-layouts: 17.7 us -> none  [the longest x9 9.29 us: near_field(): separation = neighbour[:3] + offset_vec - target]
    dot_general x22 -> x0, matrix products: 12.4 us -> none  [contract(): jnp.einsum(form, left, right, precision=lax.Precision.HIGHEST, preferred_...]
    reduce_sum x5 -> x0, other arithmetic: 9.69 us -> none  [the longest x1 5.35 us: near_field(): summed.reshape(3, planes_x, rows_y, BODIES, BODIES, cells_z).sum(axis=4)]
    add x24 -> x0, other arithmetic: 8.78 us -> none  [the longest x21 8.11 us: near_field(): separation = neighbour[:3] + offset_vec - target]
    ppermute x4 -> x0, starting transfers between devices: 7.55 us -> none  [the longest x2 7.47 us: extended_2(): lax.ppermute(head, axis, [((i + 1) % count, i) for i in range(count)])]
  transfers between devices with their start and end apart: 8 -> 0, of which waited for: 1 -> 0; matrix products, arithmetic and copies ran while one was open for 58% -> 0% of each run, Pallas kernels for 0% -> 0%
where the time goes in v1:
time: 30.6 us; the launch traced here: 30.5 us
  Pallas kernels  27.3 us (89%)
  local copies, waits for them, and re-layouts  3.09 us (10%)
    pallas_call x1, Pallas kernels, local(): pl.pallas_call(functools.partial(kernel_body, z), out_shape=jax.ShapeDtyp...  27.3 us
    unnamed x14, local copies, waits for them, and re-layouts  3.09 us

profile of v1, /device:TPU:0, one launch (start us, length us, event | category | flops | bytes accessed | tf_op | source)
XLA Modules:
  0.0 30.5 jit_solution(1070445701472143134)
XLA Ops:
  0.0 0.0 copy-start
  0.0 0.0 copy-start.1
  0.0 0.0 copy-start.2
  0.0 0.0 copy-start.3
  0.0 0.0 copy-start.5
  0.0 0.0 copy-start.4
  0.0 2.4 %copy.11 = bf16[36,2,36,1,512]{4,2,1,0,3:T(8,128)(2,1)S(1)} copy(bf16[36,2,36,1,512]{4,1,3,2,0:T(2,128)(2,1)} %param.9) | data formatting | bytes 5308416 | tf_op args[2]
  2.5 0.0 copy-done
  2.5 0.0 copy-done.1
  2.5 0.0 copy-done.2
  2.5 0.0 copy-done.3
  2.5 0.0 copy-done.5
  2.5 0.0 copy-done.4
  2.5 27.3 %shard_map.73 = f32[3,8,512]{2,1,0:T(8,128)S(1)} custom-call(f32[3,8,512]{2,1,0:T(8,128)S(1)} %bitcast.10, f32[8,512]{1,0:T(8,128)S(1)} %bitcast.11, bf16[36,2,36,512]{3,2,1,0:T(8,128)(2,1)S(1)} %bitcast.8, f32[2,1,128,128]{3,2,1,0:T(8,128)S(1)} %copy-done.3, f32[256,256]{1,0:T(8,128)S(1)} %copy-done.2, f32[256,256]{1,0:T(8,128)S(1)} %copy-done.1, ...), custom_call_target="tpu_custom_call" | custom-call | tf_op jit(solution)/shard_map/pallas_call | solution.py:535
  29.9 0.6 %copy.13 = f32[3,1,8,512]{3,2,1,0:T(8,128)} copy(f32[3,1,8,512]{3,2,1,0:T(8,128)S(1)} %bitcast.9) | data formatting | bytes 98304
Async XLA Ops:
  0.0 2.5 %copy-start = (f32[2,128,512]{2,1,0:T(8,128)S(1)}, f32[2,128,512]{2,1,0:T(8,128)}, u32[]{:S(2)}) copy-start(f32[2,128,512]{2,1,0:T(8,128)} %constant.11.clone.zi_hbm) | copy-start | bytes 1572868
  0.0 2.5 %copy-start.1 = (f32[256,256]{1,0:T(8,128)S(1)}, f32[256,256]{1,0:T(8,128)}, u32[]{:S(2)}) copy-start(f32[256,256]{1,0:T(8,128)} %constant.10.clone.xi_hbm) | copy-start | bytes 786436
  0.0 2.5 %copy-start.2 = (f32[256,256]{1,0:T(8,128)S(1)}, f32[256,256]{1,0:T(8,128)}, u32[]{:S(2)}) copy-start(f32[256,256]{1,0:T(8,128)} %constant.9.clone.xf_hbm) | copy-start | bytes 786436
  0.0 2.5 %copy-start.3 = (f32[2,1,128,128]{3,2,1,0:T(8,128)S(1)}, f32[2,1,128,128]{3,2,1,0:T(8,128)}, u32[]{:S(2)}) copy-start(f32[2,1,128,128]{3,2,1,0:T(8,128)} %constant.8.clone.zf_hbm) | copy-start | bytes 393220
  0.0 2.5 %copy-start.5 = (f32[1,8,512]{2,1,0:T(8,128)S(1)}, f32[1,8,512]{2,1,0:T(8,128)}, u32[]{:S(2)}) copy-start(f32[1,8,512]{2,1,0:T(8,128)} %param.8) | copy-start | bytes 49156
  0.0 2.5 %copy-start.4 = (f32[3,1,8,512]{3,2,1,0:T(8,128)S(1)}, f32[3,1,8,512]{3,2,1,0:T(8,128)}, u32[]{:S(2)}) copy-start(f32[3,1,8,512]{3,2,1,0:T(8,128)} %param.7) | copy-start | bytes 147460

commit v2 on v1

--- a/solution.py
+++ b/solution.py
@@ -12,8 +12,8 @@
 BODIES = 8
 SOFTEN = 0.5
 LANES = 128
+PER_STEP = 2
 MESH = pl.DeviceIdType.MESH
-HIGHEST = lax.Precision.HIGHEST
 
 
 def channel_list():
@@ -48,11 +48,18 @@
         self.prow_pad = -(-self.prow // 8) * 8
         assert planes_x == 1 and self.total_y == n_gx and rows_y == 8
         assert 2 * self.cells_z == LANES and self.q % 2 == 0
-        assert 2 * self.q * self.groups == self.total_x
+        assert 2 * self.q * self.groups == self.total_x and self.groups == 4
 
 
 def angle(left, right, length):
     return (np.multiply.outer(left, right) % length) * (2.0 * math.pi / length)
+
+
+def two_terms(table, dim):
+    table = np.asarray(table, np.float32)
+    high = table.astype(jnp.bfloat16)
+    low = (table - high.astype(np.float32)).astype(jnp.bfloat16)
+    return np.concatenate([high, low], axis=dim)
 
 
 def tables(z):
@@ -64,7 +71,7 @@
             for b in range(2):
                 zf[h, u, b, :, 0, 2 * u + b] = np.cos(ang)
                 zf[h, u, b, :, 1, 2 * u + b] = -np.sin(ang)
-    zf = zf.reshape(z.n_gy, q // 2, LANES, LANES)
+    zf = two_terms(zf.reshape(z.n_gy, q // 2, 1, LANES, LANES), 2)
     ang = angle(np.arange(nx), np.arange(nx), nx)
     c, s = np.cos(ang), np.sin(ang)
     xf = np.zeros((2, nx, wg, 2, wg, nx))
@@ -74,8 +81,8 @@
         xf[0, :, k, 1, k], xf[1, :, k, 1, k] = -s, c
         xi[0, k, :, 0, :, k], xi[1, k, :, 0, :, k] = c, -s
         xi[0, k, :, 1, :, k], xi[1, k, :, 1, :, k] = s, c
-    xf = xf.reshape(2 * LANES, 2 * LANES)
-    xi = xi.reshape(2 * LANES, 2 * LANES)
+    xf = two_terms(xf.reshape(1, 2 * LANES, 2 * LANES), 0)
+    xi = two_terms(xi.reshape(1, 2 * LANES, 2 * LANES), 0)
     zi = np.zeros((z.n_gy, 2, q, kzw, q, 2, 2, cells))
     scale = 1.0 / (z.total_x * z.total_y * cells)
     for h in range(z.n_gy):
@@ -85,12 +92,22 @@
             for copy in range(2):
                 zi[h, 0, i, :, i, 0, copy], zi[h, 1, i, :, i, 0, copy] = c, -s
                 zi[h, 0, i, :, i, 1, copy], zi[h, 1, i, :, i, 1, copy] = s, c
-    zi = zi.reshape(z.n_gy, LANES, q * 2 * LANES)
-    return [np.asarray(t, np.float32) for t in (zf, xf, xi, zi)]
+    zi = two_terms(zi.reshape(z.n_gy, 1, LANES, q * 2 * LANES), 1)
+    return zf, xf, xi, zi
+
+
+def split(value):
+    high = value.astype(jnp.bfloat16)
+    return high, (value - high.astype(jnp.float32)).astype(jnp.bfloat16)
 
 
 def dot(left, right):
-    return jnp.dot(left, right, precision=HIGHEST, preferred_element_type=jnp.float32)
+    high, low = split(left)
+
+    def one(a, b):
+        return jnp.dot(a, b, preferred_element_type=jnp.float32)
+
+    return one(high, right[0]) + (one(high, right[1]) + one(low, right[0]))
 
 
 def times_i(value, sign):
@@ -259,9 +276,9 @@
         moments_of(source, source)
     loads[2].wait()
     height = ny * z.rows_y * rows_pad
-    along = dot(mom[0].reshape(height, LANES), zf[0])
+    along = dot(mom[0].reshape(height, LANES), zf.at[0])
     for u in range(1, z.q // 2):
-        along = along + dot(mom[u].reshape(height, LANES), zf[u])
+        along = along + dot(mom[u].reshape(height, LANES), zf.at[u])
     along = [along[i * rows_pad : (i + 1) * rows_pad] for i in range(z.total_y)]
     for ky, value in enumerate(transform(along, -1.0, sign)):
         msg_b[ky] = value[:rows]
@@ -350,6 +367,7 @@
 
     lax.fori_loop(1, nx, wait_b, 0)
     groups, q = z.groups, z.q
+    deep = 2 * groups
     turned = exchange([got_b[i] for i in range(nx)], lane, z.wg)
     loads[3].wait()
     stacked = jnp.concatenate(
@@ -360,36 +378,52 @@
         ],
         axis=0,
     )
-    spectrum = dot(stacked, xf[...])
+    spectrum = dot(stacked, xf)
     for g in range(groups):
         part = spectrum[g * q * rows : g * q * rows + COUNT]
-        spec[0, g] = part[:, :LANES]
-        spec[1, g] = part[:, LANES:]
+        part_re, part_im = part[:, :LANES], part[:, LANES:]
+        for which, (front, back) in enumerate(((part_re, -part_im), (part_im, part_re))):
+            spec[which, pl.ds(2 * g, COUNT, stride=deep), :] = front
+            spec[which, pl.ds(2 * g + 1, COUNT, stride=deep), :] = back
     loads[6].wait()
-    for g in range(groups):
-        lanes = slice(g * LANES, (g + 1) * LANES)
-        spec_re, spec_im = spec[0, g], spec[1, g]
-
-        def couple(d, carry):
-            gain_re = gain[d, 0, :, lanes].astype(jnp.float32)
-            gain_im = gain[d, 1, :, lanes].astype(jnp.float32)
-            coef[0, g, pl.ds(d, 1), :] = jnp.sum(gain_re * spec_re - gain_im * spec_im, axis=0, keepdims=True)
-            coef[1, g, pl.ds(d, 1), :] = jnp.sum(gain_re * spec_im + gain_im * spec_re, axis=0, keepdims=True)
-            return carry
-
-        lax.fori_loop(0, COUNT, couple, 0, unroll=6)
+
+    def couple(step, carry):
+        members = [step * PER_STEP + i for i in range(PER_STEP)]
+        sums = [[None, None] for _ in range(2 * PER_STEP)]
+        for c in range(0, COUNT, 2):
+            spec_two = [[spec[w, (c + i) * deep : (c + i + 1) * deep] for w in range(2)] for i in range(2)]
+            for n in range(2 * PER_STEP):
+                d = members[n // 2] + (n % 2) * HALF
+                two = gain[d, c * deep : (c + 2) * deep, :].astype(jnp.float32)
+                for i in range(2):
+                    one = two[i * deep : (i + 1) * deep]
+                    for w in range(2):
+                        term = one * spec_two[i][w]
+                        sums[n][w] = term if sums[n][w] is None else sums[n][w] + term
+        for i, p in enumerate(members):
+            own, other = sums[2 * i], sums[2 * i + 1]
+            start = pl.multiple_of(p * deep, deep)
+            coef[0, pl.ds(start, deep), :] = own[0] - other[1]
+            coef[1, pl.ds(start, deep), :] = own[1] + other[0]
+        return carry
+
+    lax.fori_loop(0, HALF // PER_STEP, couple, 0)
     prow = z.prow
     height = q * prow
     pairs = []
     for g in range(groups):
-        pair_re = coef[0, g, :HALF] - coef[1, g, HALF:]
-        pair_im = coef[1, g, :HALF] + coef[0, g, HALF:]
-        pair = jnp.concatenate([pair_re, pair_im], axis=1)
+        pair = jnp.concatenate(
+            [
+                coef[w, pl.ds(2 * g, HALF, stride=deep), :] + coef[w, pl.ds(2 * g + 1, HALF, stride=deep), :]
+                for w in range(2)
+            ],
+            axis=1,
+        )
         if height > HALF:
             pair = jnp.concatenate([pair, jnp.zeros((height - HALF, 2 * LANES), jnp.float32)], axis=0)
         pairs.append(pair)
     loads[4].wait()
-    back = dot(jnp.concatenate(pairs, axis=0), xi[...])
+    back = dot(jnp.concatenate(pairs, axis=0), xi)
     ordered = [
         back[g * height + i * prow : g * height + (i + 1) * prow, ri * LANES : (ri + 1) * LANES]
         for ri in range(2)
@@ -430,7 +464,7 @@
         for y, value in enumerate(transform([got_c[h, k] for k in range(nx)], 1.0, sign)):
             lines[h, y, :prow] = value
         own = lines[h, pl.ds(my * z.rows_y, z.rows_y)].reshape(z.rows_y * prow_pad, LANES)
-        term = dot(own, zi[h])
+        term = dot(own, zi.at[h])
         result = term if result is None else result + term
     for column, tile in enumerate(lane_tiles(result)):
         field[column] = tile
@@ -495,16 +529,16 @@
     waves = kernel.shape[3] * kernel.shape[4]
     z = Sizes(n_gx, n_gy, planes_x, rows_y, width, waves)
     made = tables(z)
-    f32 = jnp.float32
+    f32, bf16 = jnp.float32, jnp.bfloat16
     tiles = width // LANES
     scratch = [
         pltpu.VMEM((3, rows_y, width), f32),
         pltpu.VMEM((rows_y, width), f32),
-        pltpu.VMEM((COUNT, 2, COUNT, waves), kernel.dtype),
-        pltpu.VMEM(made[0].shape[1:], f32),
-        pltpu.VMEM(made[1].shape, f32),
-        pltpu.VMEM(made[2].shape, f32),
-        pltpu.VMEM(made[3].shape, f32),
+        pltpu.VMEM((COUNT, COUNT * 2 * z.groups, LANES), kernel.dtype),
+        pltpu.VMEM(made[0].shape[1:], bf16),
+        pltpu.VMEM(made[1].shape, bf16),
+        pltpu.VMEM(made[2].shape, bf16),
+        pltpu.VMEM(made[3].shape, bf16),
         pltpu.VMEM((n_gy, 4, rows_y, width), f32),
         pltpu.VMEM((2, 4, 1, width), f32),
         pltpu.VMEM((2, 4, rows_y, width), f32),
@@ -514,8 +548,8 @@
         pltpu.VMEM((z.q // 2, n_gy, rows_y * z.rows_pad, LANES), f32),
         pltpu.VMEM((n_gx, z.rows, LANES), f32),
         pltpu.VMEM((n_gx, z.rows, LANES), f32),
-        pltpu.VMEM((2, z.groups, COUNT, LANES), f32),
-        pltpu.VMEM((2, z.groups, COUNT, LANES), f32),
+        pltpu.VMEM((2, COUNT * 2 * z.groups, LANES), f32),
+        pltpu.VMEM((2, HALF * 2 * z.groups, LANES), f32),
         pltpu.VMEM((n_gx, z.prow, LANES), f32),
         pltpu.VMEM((n_gy, n_gx, z.prow, LANES), f32),
         pltpu.VMEM((n_gy, n_gx, z.prow_pad, LANES), f32),
@@ -532,18 +566,20 @@
         pltpu.SemaphoreType.DMA((n_gy, n_gx)),
         pltpu.SemaphoreType.DMA((n_gy, n_gx)),
     ]
+    gains = jnp.transpose(kernel.reshape(COUNT, 2, COUNT, z.groups, LANES), (0, 2, 3, 1, 4))
+    gains = gains.reshape(COUNT, COUNT * 2 * z.groups, LANES)
     out = pl.pallas_call(
         functools.partial(kernel_body, z),
         out_shape=jax.ShapeDtypeStruct((3, rows_y, width), f32),
-        in_specs=[pl.BlockSpec(memory_space=pl.ANY)] * 7,
+        in_specs=[pl.BlockSpec(memory_space=pltpu.HBM)] * 7,
         out_specs=pl.BlockSpec(memory_space=pltpu.VMEM),
         scratch_shapes=scratch,
         compiler_params=pltpu.CompilerParams(
-            collective_id=0, has_side_effects=True, vmem_limit_bytes=48 * 1024 * 1024
+            collective_id=0, has_side_effects=True, vmem_limit_bytes=62 * 1024 * 1024
         ),
     )(
         offsets.reshape(3, rows_y, width), masses.reshape(rows_y, width),
-        kernel.reshape(COUNT, 2, COUNT, waves), *[jnp.asarray(t) for t in made],
+        gains, *[jnp.asarray(t) for t in made],
     )
     return out.reshape(3, planes_x, rows_y, width)
 

time: 30.6 us -> 28.2 us (0.922)
  local copies, waits for them, and re-layouts: 3.09 us -> 1.42 us
  Pallas kernels: 27.3 us -> 26.6 us
    unnamed x14 -> x1, local copies, waits for them, and re-layouts: 3.09 us -> 1.42 us
    pallas_call x1, Pallas kernels: 27.3 us -> 26.6 us  [local(): pl.pallas_call(functools.partial(kernel_body, z), out_shape=jax.ShapeDtyp...]
where the time goes in v2:
time: 28.2 us; the launch traced here: 28.1 us
  Pallas kernels  26.6 us (94%)
  local copies, waits for them, and re-layouts  1.42 us (5%)
    pallas_call x1, Pallas kernels, local(): pl.pallas_call(functools.partial(kernel_body, z), out_shape=jax.ShapeDtyp...  26.6 us
    unnamed x1, local copies, waits for them, and re-layouts  1.42 us

profile of v2, /device:TPU:0, one launch (start us, length us, event | category | flops | bytes accessed | tf_op | source)
XLA Modules:
  0.0 28.1 jit_solution(111289637032644142)
XLA Ops:
  0.0 26.6 %shard_map.73 = f32[3,8,512]{2,1,0:T(8,128)} custom-call(f32[3,8,512]{2,1,0:T(8,128)} %bitcast.12, f32[8,512]{1,0:T(8,128)} %bitcast.13, bf16[36,288,128]{2,1,0:T(8,128)(2,1)} %bitcast.10, bf16[2,1,2,128,128]{4,3,2,1,0:T(8,128)(2,1)} %constant.8.clone.zf_hbm, bf16[2,256,256]{2,1,0:T(8,128)(2,1)} %constant.9.clone.xf_hbm, ...), custom_call_target="tpu_custom_call" | custom-call | tf_op jit(solution)/shard_map/pallas_call | solution.py:571
  26.6 1.4 %copy.11 = f32[3,1,8,512]{3,2,1,0:T(8,128)} copy(f32[3,1,8,512]{3,2,1,0:T(8,128)} %bitcast.11) | data formatting | bytes 98304

commit v3 on v2

--- a/solution.py
+++ b/solution.py
@@ -174,16 +174,27 @@
     me = mx * ny + my
     total = nx * ny
 
-    def peer(k):
-        other = lax.rem(me + k, total)
-        return other // ny, lax.rem(other, ny)
+    def wrap(index, count):
+        return jnp.where(index >= count, index - count, index)
+
+    def each_peer(act):
+        for j in range(ny):
+            py = wrap(my + j, ny)
+
+            def body(k, carry):
+                act(wrap(mx + k, nx), py)
+                return carry
+
+            lax.fori_loop(0 if j else 1, nx, body, 0)
+
+    def all_of(buffer, count, sem):
+        span = buffer.at[pl.ds(0, count)]
+        pltpu.make_async_copy(span, span, sem).wait()
 
     barrier = pltpu.get_barrier_semaphore()
 
-    def greet(k, carry):
-        px, py = peer(k)
+    def greet(px, py):
         pl.semaphore_signal(barrier, inc=1, device_id=(px, py), device_id_type=MESH)
-        return carry
 
     loads = [
         pltpu.make_async_copy(src, dst, load_sem.at[i])
@@ -194,7 +205,7 @@
     ]
     for load in loads:
         load.start()
-    lax.fori_loop(1, total, greet, 0)
+    each_peer(greet)
     loads[0].wait()
     loads[1].wait()
 
@@ -283,10 +294,12 @@
     for ky, value in enumerate(transform(along, -1.0, sign)):
         msg_b[ky] = value[:rows]
 
+    stride = 5 if nx % 5 else 1
+
     def send_b(k, carry):
-        to = lax.rem(mx + k, nx)
+        to = lax.rem(mx + stride * k, nx)
         pltpu.make_async_remote_copy(
-            src_ref=msg_b.at[to], dst_ref=got_b.at[mx], send_sem=bsend.at[to], recv_sem=brecv.at[mx],
+            src_ref=msg_b.at[to], dst_ref=got_b.at[mx], send_sem=bsend, recv_sem=brecv,
             device_id=(to, my), device_id_type=MESH,
         ).start()
         return carry
@@ -357,15 +370,7 @@
         fill(2 * side, lambda comp: xh[side, comp], lambda comp: xc[side, 0, comp], lambda comp: xc[side, 1, comp])
     near_steps(0, 3 * tiles)
 
-    def wait_b(k, carry):
-        source = lax.rem(mx + k, nx)
-        pltpu.make_async_remote_copy(
-            src_ref=msg_b.at[source], dst_ref=got_b.at[source], send_sem=bsend.at[source],
-            recv_sem=brecv.at[source], device_id=(source, my), device_id_type=MESH,
-        ).wait_recv()
-        return carry
-
-    lax.fori_loop(1, nx, wait_b, 0)
+    all_of(got_b, nx - 1, brecv)
     groups, q = z.groups, z.q
     deep = 2 * groups
     turned = exchange([got_b[i] for i in range(nx)], lane, z.wg)
@@ -433,35 +438,25 @@
     for x, value in enumerate(exchange(ordered, lane, z.wg)):
         msg_c[x] = value
 
-    def send_c(k, carry):
-        px, py = peer(k)
+    def send_c(px, py):
         pltpu.make_async_remote_copy(
-            src_ref=msg_c.at[px], dst_ref=got_c.at[my, mx], send_sem=fsend.at[py, px], recv_sem=frecv.at[my, mx],
+            src_ref=msg_c.at[px], dst_ref=got_c.at[me], send_sem=fsend, recv_sem=frecv,
             device_id=(px, py), device_id_type=MESH,
         ).start()
-        return carry
-
-    lax.fori_loop(1, total, send_c, 0)
-    got_c[my, mx] = msg_c[mx]
+
+    each_peer(send_c)
+    got_c[me] = msg_c[mx]
 
     near_steps(6 * tiles, 9 * tiles)
 
-    def wait_c(k, carry):
-        px, py = peer(k)
-        pltpu.make_async_remote_copy(
-            src_ref=msg_c.at[px], dst_ref=got_c.at[py, px], send_sem=fsend.at[py, px], recv_sem=frecv.at[py, px],
-            device_id=(px, py), device_id_type=MESH,
-        ).wait_recv()
-        return carry
-
-    lax.fori_loop(1, total, wait_c, 0)
+    all_of(got_c, total - 1, frecv)
     loads[5].wait()
     prow_pad = z.prow_pad
     if prow_pad != prow:
         lines[:, :, prow:, :] = jnp.zeros(lines.shape[:2] + (prow_pad - prow, LANES), jnp.float32)
     result = None
     for h in range(ny):
-        for y, value in enumerate(transform([got_c[h, k] for k in range(nx)], 1.0, sign)):
+        for y, value in enumerate(transform([got_c[k * ny + h] for k in range(nx)], 1.0, sign)):
             lines[h, y, :prow] = value
         own = lines[h, pl.ds(my * z.rows_y, z.rows_y)].reshape(z.rows_y * prow_pad, LANES)
         term = dot(own, zi.at[h])
@@ -502,25 +497,8 @@
     for copy in h_copies:
         copy.wait_send()
 
-    def drain_b(k, carry):
-        to = lax.rem(mx + k, nx)
-        pltpu.make_async_remote_copy(
-            src_ref=msg_b.at[to], dst_ref=got_b.at[mx], send_sem=bsend.at[to], recv_sem=brecv.at[mx],
-            device_id=(to, my), device_id_type=MESH,
-        ).wait_send()
-        return carry
-
-    lax.fori_loop(1, nx, drain_b, 0)
-
-    def drain_c(k, carry):
-        px, py = peer(k)
-        pltpu.make_async_remote_copy(
-            src_ref=msg_c.at[px], dst_ref=got_c.at[my, mx], send_sem=fsend.at[py, px], recv_sem=frecv.at[my, mx],
-            device_id=(px, py), device_id_type=MESH,
-        ).wait_send()
-        return carry
-
-    lax.fori_loop(1, total, drain_c, 0)
+    all_of(got_b, nx - 1, bsend)
+    all_of(got_c, total - 1, fsend)
 
 
 def local(offsets, masses, kernel):
@@ -551,7 +529,7 @@
         pltpu.VMEM((2, COUNT * 2 * z.groups, LANES), f32),
         pltpu.VMEM((2, HALF * 2 * z.groups, LANES), f32),
         pltpu.VMEM((n_gx, z.prow, LANES), f32),
-        pltpu.VMEM((n_gy, n_gx, z.prow, LANES), f32),
+        pltpu.VMEM((n_gy * n_gx, z.prow, LANES), f32),
         pltpu.VMEM((n_gy, n_gx, z.prow_pad, LANES), f32),
         pltpu.VMEM((z.q * 2, rows_y * z.prow_pad, LANES), f32),
         pltpu.SemaphoreType.DMA((7,)),
@@ -561,10 +539,10 @@
         pltpu.SemaphoreType.DMA((2,)),
         pltpu.SemaphoreType.DMA((2, 2)),
         pltpu.SemaphoreType.DMA((2, 2)),
-        pltpu.SemaphoreType.DMA((n_gx,)),
-        pltpu.SemaphoreType.DMA((n_gx,)),
-        pltpu.SemaphoreType.DMA((n_gy, n_gx)),
-        pltpu.SemaphoreType.DMA((n_gy, n_gx)),
+        pltpu.SemaphoreType.DMA,
+        pltpu.SemaphoreType.DMA,
+        pltpu.SemaphoreType.DMA,
+        pltpu.SemaphoreType.DMA,
     ]
     gains = jnp.transpose(kernel.reshape(COUNT, 2, COUNT, z.groups, LANES), (0, 2, 3, 1, 4))
     gains = gains.reshape(COUNT, COUNT * 2 * z.groups, LANES)

time: 28.2 us -> 27.5 us (0.975)
  Pallas kernels: 26.6 us -> 25.9 us
    pallas_call x1, Pallas kernels: 26.6 us -> 25.9 us  [local(): pl.pallas_call(functools.partial(kernel_body, z), out_shape=jax.ShapeDtyp...]
where the time goes in v3:
time: 27.5 us; the launch traced here: 27.3 us
  Pallas kernels  25.9 us (94%)
  local copies, waits for them, and re-layouts  1.42 us (5%)
    pallas_call x1, Pallas kernels, local(): pl.pallas_call(functools.partial(kernel_body, z), out_shape=jax.ShapeDtyp...  25.9 us
    unnamed x1, local copies, waits for them, and re-layouts  1.42 us

profile of v3, /device:TPU:0, one launch (start us, length us, event | category | flops | bytes accessed | tf_op | source)
XLA Modules:
  0.0 27.3 jit_solution(2251281760948985894)
XLA Ops:
  0.0 25.9 %shard_map.73 = f32[3,8,512]{2,1,0:T(8,128)} custom-call(f32[3,8,512]{2,1,0:T(8,128)} %bitcast.12, f32[8,512]{1,0:T(8,128)} %bitcast.13, bf16[36,288,128]{2,1,0:T(8,128)(2,1)} %bitcast.10, bf16[2,1,2,128,128]{4,3,2,1,0:T(8,128)(2,1)} %constant.8.clone.zf_hbm, bf16[2,256,256]{2,1,0:T(8,128)(2,1)} %constant.9.clone.xf_hbm, ...), custom_call_target="tpu_custom_call" | custom-call | tf_op jit(solution)/shard_map/pallas_call | solution.py:549
  25.9 1.4 %copy.11 = f32[3,1,8,512]{3,2,1,0:T(8,128)} copy(f32[3,1,8,512]{3,2,1,0:T(8,128)} %bitcast.11) | data formatting | bytes 98304

commit v4 on v3

--- a/solution.py
+++ b/solution.py
@@ -287,9 +287,9 @@
         moments_of(source, source)
     loads[2].wait()
     height = ny * z.rows_y * rows_pad
-    along = dot(mom[0].reshape(height, LANES), zf.at[0])
+    along = dot(mom[0, :ny].reshape(height, LANES), zf.at[0])
     for u in range(1, z.q // 2):
-        along = along + dot(mom[u].reshape(height, LANES), zf.at[u])
+        along = along + dot(mom[u, :ny].reshape(height, LANES), zf.at[u])
     along = [along[i * rows_pad : (i + 1) * rows_pad] for i in range(z.total_y)]
     for ky, value in enumerate(transform(along, -1.0, sign)):
         msg_b[ky] = value[:rows]
@@ -462,7 +462,7 @@
         term = dot(own, zi.at[h])
         result = term if result is None else result + term
     for column, tile in enumerate(lane_tiles(result)):
-        field[column] = tile
+        field[column, : z.rows_y * prow_pad] = tile
 
     def coefficient(c):
         part, p = c // HALF, c % HALF
@@ -523,15 +523,15 @@
         pltpu.VMEM((2, 2, 4, 1, width), f32),
         pltpu.VMEM((9 * tiles, 4, rows_y, LANES), f32),
         pltpu.VMEM((3, rows_y, width), f32),
-        pltpu.VMEM((z.q // 2, n_gy, rows_y * z.rows_pad, LANES), f32),
+        pltpu.VMEM((z.q // 2, n_gy + 1, rows_y * z.rows_pad, LANES), f32),
         pltpu.VMEM((n_gx, z.rows, LANES), f32),
         pltpu.VMEM((n_gx, z.rows, LANES), f32),
-        pltpu.VMEM((2, COUNT * 2 * z.groups, LANES), f32),
-        pltpu.VMEM((2, HALF * 2 * z.groups, LANES), f32),
+        pltpu.VMEM((2, -(-COUNT // 8) * 16 * z.groups, LANES), f32),
+        pltpu.VMEM((2, -(-HALF // 8) * 16 * z.groups, LANES), f32),
         pltpu.VMEM((n_gx, z.prow, LANES), f32),
         pltpu.VMEM((n_gy * n_gx, z.prow, LANES), f32),
         pltpu.VMEM((n_gy, n_gx, z.prow_pad, LANES), f32),
-        pltpu.VMEM((z.q * 2, rows_y * z.prow_pad, LANES), f32),
+        pltpu.VMEM((z.q * 2, (rows_y + 1) * z.prow_pad, LANES), f32),
         pltpu.SemaphoreType.DMA((7,)),
         pltpu.SemaphoreType.DMA((n_gy,)),
         pltpu.SemaphoreType.DMA((n_gy,)),

time: 27.5 us -> 27.5 us (level)
  no operation moved by 1% of the time
where the time goes in v4:
time: 27.5 us; the launch traced here: 27.3 us
  Pallas kernels  25.9 us (94%)
  local copies, waits for them, and re-layouts  1.42 us (5%)
    pallas_call x1, Pallas kernels, local(): pl.pallas_call(functools.partial(kernel_body, z), out_shape=jax.ShapeDtyp...  25.9 us
    unnamed x1, local copies, waits for them, and re-layouts  1.42 us

profile of v4, /device:TPU:0, one launch (start us, length us, event | category | flops | bytes accessed | tf_op | source)
XLA Modules:
  0.0 27.3 jit_solution(16325612337441728377)
XLA Ops:
  0.0 25.9 %shard_map.73 = f32[3,8,512]{2,1,0:T(8,128)} custom-call(f32[3,8,512]{2,1,0:T(8,128)} %bitcast.12, f32[8,512]{1,0:T(8,128)} %bitcast.13, bf16[36,288,128]{2,1,0:T(8,128)(2,1)} %bitcast.10, bf16[2,1,2,128,128]{4,3,2,1,0:T(8,128)(2,1)} %constant.8.clone.zf_hbm, bf16[2,256,256]{2,1,0:T(8,128)(2,1)} %constant.9.clone.xf_hbm, ...), custom_call_target="tpu_custom_call" | custom-call | tf_op jit(solution)/shard_map/pallas_call | solution.py:549
  25.9 1.4 %copy.11 = f32[3,1,8,512]{3,2,1,0:T(8,128)} copy(f32[3,1,8,512]{3,2,1,0:T(8,128)} %bitcast.11) | data formatting | bytes 98304
